TPU v7x, 32 devices: a whole 2x2x4 slice. The times are simulated.
32 devices in a mesh: parts: 2 (over x), row: 4 (over y, core), col: 4 (over z).
Axes of the slice: x: 2, y: 2, z: 4, core: 2. Of those that a mesh axis runs over, the one named last changes fastest.
Arguments:
- pair: bfloat16 [192, 96, 128], P(('parts', 'row'), 'col'), parts along dimension 0, may hold values from -6 to 6
- atom_feats: bfloat16 [3072, 128], P(('parts', 'row', 'col')), parts along dimension 0, may hold values from -6 to 6
- atom_token: int32 [3072], P(('parts', 'row', 'col')), parts along dimension 0, may hold values from 0 to 95, never falling along the last dimension, each value on 1 to 32 neighbouring positions
- atom_mask: int32 [3072], P(('parts', 'row', 'col')), parts along dimension 0, may hold values 0 or 1
- token_mask: int32 [192], P('parts'), parts along dimension 0, may hold values 0 or 1
- w_atom: bfloat16 [128, 384], replicated, may hold values from -0.5 to 0.5
- gain_single: float32 [384], replicated, may hold values from 0.25 to 1.75
- w_rows: bfloat16 [384, 128], replicated, may hold values from -0.3125 to 0.3125
- w_cols: bfloat16 [384, 128], replicated, may hold values from -0.3125 to 0.3125
- gain_pair: float32 [128], replicated, may hold values from 0.25 to 1.75
- w_left: bfloat16 [128, 128], replicated, may hold values from -0.5 to 0.5
- w_left_gate: bfloat16 [128, 128], replicated, may hold values from -0.5 to 0.5
- w_right: bfloat16 [128, 128], replicated, may hold values from -0.5 to 0.5
- w_right_gate: bfloat16 [128, 128], replicated, may hold values from -0.5 to 0.5
- w_out_gate: bfloat16 [128, 128], replicated, may hold values from -0.5 to 0.5
- gain_tri: float32 [128], replicated, may hold values from 0.25 to 1.75
- w_out: bfloat16 [128, 128], replicated, may hold values from -0.5 to 0.5
- gain_trans: float32 [128], replicated, may hold values from 0.25 to 1.75
- w_up: bfloat16 [128, 512], replicated, may hold values from -0.5 to 0.5
- w_upgate: bfloat16 [128, 512], replicated, may hold values from -0.5 to 0.5
- w_down: bfloat16 [512, 128], replicated, may hold values from -0.25 to 0.25
Outputs:
- pair_out: bfloat16 [192, 96, 128], P(('parts', 'row'), 'col'), parts along dimension 0
There are 2 independent parts, one for each index of `parts`. A program takes and returns all parts, laid end to end along the dimension named above; an argument that names none is the same for every part. Nothing has to cross between parts.
Inputs may be any that keep to these rules, and one draw needn't show every extreme that they name: `atom_token`: never falls along the atoms; every token has 1 to 32 atoms, and some token exactly 32.
All inputs are finite; a program needn't handle non-finite values. No bound on the sum of `atom_mask` on one device may be relied on, other than what follows from the above.
Results may differ from a plain program's by a relative error of at most 0.005.
Values may be sent and summed in bfloat16 or wider, within the bound.
A program may use at most 128 MiB of HBM per device.

v0:
```python
import jax
import jax.numpy as jnp
from jax import lax
from jax.sharding import PartitionSpec as P

norm_epsilon = 1e-05


def layer_norm(values, gain_vec):
    centre = jnp.mean(values, axis=-1, keepdims=True)
    centered = values - centre
    variance = jnp.mean(centered * centered, axis=-1, keepdims=True)
    return centered * lax.rsqrt(variance + norm_epsilon) * gain_vec


def gated_proj(values, w_value, w_gate, pair_weight):
    gate_part = jax.nn.sigmoid(jnp.dot(values, w_gate, preferred_element_type=jnp.float32))
    value_part = jnp.dot(values, w_value, preferred_element_type=jnp.float32)
    return (gate_part * value_part * pair_weight[..., None]).astype(jnp.bfloat16)


def per_device(
    pair,
    atom_feats,
    atom_token,
    atom_mask,
    token_mask,
    w_atom,
    gain_single,
    w_rows,
    w_cols,
    gain_pair,
    w_left,
    w_left_gate,
    w_right,
    w_right_gate,
    w_out_gate,
    gain_tri,
    w_out,
    gain_trans,
    w_up,
    w_upgate,
    w_down,
):
    highest = lax.Precision.HIGHEST
    row_count = lax.axis_size("row")
    col_count = lax.axis_size("col")
    row_index = lax.axis_index("row")
    col_index = lax.axis_index("col")
    rows_blk, cols_blk, channels = pair.shape
    tokens = token_mask.shape[0]
    member = (jnp.arange(tokens, dtype=jnp.int32)[:, None] == atom_token[None, :]).astype(
        jnp.float32
    )
    member = member * atom_mask.astype(jnp.float32)[None, :]
    projected = jnp.dot(atom_feats, w_atom, preferred_element_type=jnp.float32)
    partial_sums = jnp.dot(member, projected, precision=highest)
    total_sums = lax.psum(partial_sums, ("row", "col"))
    single = layer_norm(total_sums, gain_single)
    single_rows = lax.dynamic_slice_in_dim(single, row_index * rows_blk, rows_blk, 0)
    single_cols = lax.dynamic_slice_in_dim(single, col_index * cols_blk, cols_blk, 0)
    row_term = jnp.dot(single_rows, w_rows.astype(jnp.float32), precision=highest)
    col_term = jnp.dot(single_cols, w_cols.astype(jnp.float32), precision=highest)
    z_first = pair.astype(jnp.float32) + row_term[:, None, :] + col_term[None, :, :]
    normed_pair = layer_norm(z_first, gain_pair).astype(jnp.bfloat16)
    mask_all = token_mask.astype(jnp.float32)
    mask_rows = lax.dynamic_slice_in_dim(mask_all, row_index * rows_blk, rows_blk, 0)
    mask_cols = lax.dynamic_slice_in_dim(mask_all, col_index * cols_blk, cols_blk, 0)
    pair_weight = mask_rows[:, None] * mask_cols[None, :]
    left = gated_proj(normed_pair, w_left, w_left_gate, pair_weight)
    right = gated_proj(normed_pair, w_right, w_right_gate, pair_weight)
    out_gate = jax.nn.sigmoid(jnp.dot(normed_pair, w_out_gate, preferred_element_type=jnp.float32))
    sub_rows = rows_blk // col_count
    shaped = left.reshape(sub_rows, col_count, cols_blk, channels)
    moved = lax.all_to_all(
        lax.all_to_all(shaped, "col", split_axis=1, concat_axis=2, tiled=True),
        "row",
        split_axis=2,
        concat_axis=0,
        tiled=True,
    )
    moved = moved.reshape(row_count, sub_rows, 1, rows_blk, channels)
    left_all = lax.all_gather(moved, "col", axis=2, tiled=True).reshape(tokens, rows_blk, channels)
    triangle = jnp.einsum(
        "kic,kjc->ijc",
        left_all,
        lax.all_gather(right, "row", axis=0, tiled=True),
        preferred_element_type=jnp.float32,
    )
    tri_normed = layer_norm(triangle, gain_tri).astype(jnp.bfloat16)
    z_second = z_first + jnp.dot(tri_normed, w_out, preferred_element_type=jnp.float32) * out_gate
    trans_in = layer_norm(z_second, gain_trans).astype(jnp.bfloat16)
    hidden = (
        jax.nn.silu(jnp.dot(trans_in, w_upgate, preferred_element_type=jnp.float32))
        * jnp.dot(trans_in, w_up, preferred_element_type=jnp.float32)
    ).astype(jnp.bfloat16)
    return (z_second + jnp.dot(hidden, w_down, preferred_element_type=jnp.float32)).astype(
        jnp.bfloat16
    )


def solution(mesh):
    placed = (
        P(("parts", "row"), "col", None),
        P(("parts", "row", "col"), None),
        P(("parts", "row", "col")),
        P(("parts", "row", "col")),
        P("parts"),
        P(),
        P(),
        P(),
        P(),
        P(),
        P(),
        P(),
        P(),
        P(),
        P(),
        P(),
        P(),
        P(),
        P(),
        P(),
        P(),
    )
    return jax.shard_map(
        per_device,
        mesh=mesh,
        in_specs=placed,
        out_specs=P(("parts", "row"), "col", None),
        check_vma=False,
    )
```

profile of v0, /device:TPU:0, one launch (start us, length us, event | category | flops | bytes accessed | tf_op | source)
XLA Modules:
  0.0 160.9 jit_solution(14069623892460264347)
XLA Ops:
  6.6 0.8 convert_element_type.34
  7.4 1.1 fusion.64
  8.4 1.6 fusion.43
  10.0 0.7 convert_element_type.36
  10.9 90.5 %all-reduce.2.cloned.1.call-done = f32[96,384]{1,0:T(8,128)} async-done(((f32[96,384]{1,0:T(8,128)}), f32[96,384]{1,0:T(8,128)}) %all-reduce.2.cloned.1.call-update) | async-done | bytes 147472 | tf_op jit(solution)/shard_map/psum | solution.py:58
  101.3 1.0 reduce_sum.72
  102.4 1.1 multiply_reduce_fusion.3
  103.5 1.0 multiply_multiply_fusion
  104.7 0.2 fusion.45
  105.0 0.3 multiply_reduce_fusion.2
  105.4 0.4 fusion.15
  105.8 0.4 fusion.22
  106.1 0.7 copy.69
  106.8 5.5 %all-to-all-start = ((bf16[6,4,24,128]{3,2,0,1:T(8,128)(2,1)}), bf16[6,4,24,128]{3,2,0,1:T(8,128)(2,1)S(1)}, u32[]{:S(2)}, u32[]{:S(2)}) async-start(bf16[6,4,24,128]{3,2,0,1:T(8,128)(2,1)} %copy.69), calls=%async_computation | async-start | bytes 294912 | tf_op jit(solution)/shard_map/all_to_all | solution.py:76
  112.3 0.4 fusion.18
  112.7 0.4 fusion.21
  113.1 1.1 fusion.12
  114.2 4.1 %all-to-all-done = bf16[6,4,24,128]{3,2,0,1:T(8,128)(2,1)S(1)} async-done(((bf16[6,4,24,128]{3,2,0,1:T(8,128)(2,1)}), bf16[6,4,24,128]{3,2,0,1:T(8,128)(2,1)S(1)}, u32[]{:S(2)}, u32[]{:S(2)}) %all-to-all-start) | async-done | bytes 147488 | tf_op jit(solution)/shard_map/all_to_all | solution.py:76
  118.3 0.7 copy.71
  119.0 3.4 %all-to-all-start.1 = ((bf16[6,1,96,128]{3,0,1,2:T(8,128)(2,1)}), bf16[6,1,96,128]{3,0,1,2:T(8,128)(2,1)S(1)}, u32[]{:S(2)}, u32[]{:S(2)}) async-start(bf16[6,1,96,128]{3,0,1,2:T(8,128)(2,1)} %copy.71), calls=%async_computation.1 | async-start | bytes 393216 | tf_op jit(solution)/shard_map/all_to_all | solution.py:75
  122.4 9.3 %all_gather.6 = bf16[96,24,128]{2,1,0:T(8,128)(2,1)S(1)} all-gather(bf16[24,24,128]{2,1,0:T(8,128)(2,1)S(1)} %fusion.21), channel_id=1, replica_groups=mesh['parts'=2,'row'=4,'col'=4] {'row'}, dimensions={0}, use_global_device_ids=true | all-gather | bytes 737280 | tf_op jit(solution)/shard_map/all_gather | solution.py:87
  131.7 0.6 copy.75
  132.4 16.7 %all_gather.7 = bf16[4,6,4,24,128]{4,3,1,0,2:T(8,128)(2,1)S(1)} all-gather(bf16[4,6,1,24,128]{4,3,1,0,2:T(8,128)(2,1)S(1)} %copy.73), channel_id=1, replica_groups=mesh['parts'=2,'row'=4,'col'=4] {'col'}, dimensions={2}, use_global_device_ids=true | all-gather | bytes 737280 | tf_op jit(solution)/shard_map/all_gather | solution.py:83
  149.2 0.6 copy.76
  149.8 0.5 bitcast_reduce_fusion
  150.3 0.5 copy.77
  150.9 0.3 multiply_reduce_fusion.1
  151.3 0.4 fusion.63
  151.7 0.3 multiply_reduce_fusion
  152.1 0.4 fusion.26
  152.4 0.2 copy-done.8
  152.7 1.3 fusion.20
  (51 shorter events, 1.0 us)
Async XLA Ops:
  6.5 145.5 %copy-start = (bf16[128,512]{1,0:T(8,128)(2,1)S(1)}, bf16[128,512]{1,0:T(8,128)(2,1)}, u32[]{:S(2)}) copy-start(bf16[128,512]{1,0:T(8,128)(2,1)} %param.40) | copy-start | bytes 393220
  6.5 98.0 %copy-start.3 = (bf16[384,128]{1,0:T(8,128)(2,1)S(1)}, bf16[384,128]{1,0:T(8,128)(2,1)}, u32[]{:S(2)}) copy-start(bf16[384,128]{1,0:T(8,128)(2,1)} %param.28) | copy-start | bytes 294916
  6.5 98.1 %copy-start.4 = (bf16[384,128]{1,0:T(8,128)(2,1)S(1)}, bf16[384,128]{1,0:T(8,128)(2,1)}, u32[]{:S(2)}) copy-start(bf16[384,128]{1,0:T(8,128)(2,1)} %param.29) | copy-start | bytes 294916
  6.5 98.3 %copy-start.1 = (bf16[24,24,128]{2,1,0:T(8,128)(2,1)S(1)}, bf16[24,24,128]{2,1,0:T(8,128)(2,1)}, u32[]{:S(2)}) copy-start(bf16[24,24,128]{2,1,0:T(8,128)(2,1)} %param.21) | copy-start | bytes 442372
  6.5 98.8 %copy-start.15 = (f32[128]{0:T(128)S(1)}, f32[128]{0:T(128)}, u32[]{:S(2)}) copy-start(f32[128]{0:T(128)} %param.30) | copy-start | bytes 1540
  6.5 98.8 %copy-start.10 = (bf16[128,128]{1,0:T(8,128)(2,1)S(1)}, bf16[128,128]{1,0:T(8,128)(2,1)}, u32[]{:S(2)}) copy-start(bf16[128,128]{1,0:T(8,128)(2,1)} %param.32) | copy-start | bytes 98308
  6.6 94.8 %all-reduce.2.cloned.1.call-start = ((), (), s32[]{:S(2)}) async-start(), calls=%async_computation.2 | async-start | bytes 294912 | tf_op jit(solution)/shard_map/psum | solution.py:58
  104.7 1.1 copy-start.11
  105.4 7.0 %copy-start.12 = (bf16[128,128]{1,0:T(8,128)(2,1)S(1)}, bf16[128,128]{1,0:T(8,128)(2,1)}, u32[]{:S(2)}) copy-start(bf16[128,128]{1,0:T(8,128)(2,1)} %param.34) | copy-start | bytes 98308
  106.1 6.6 %copy-start.13 = (bf16[128,128]{1,0:T(8,128)(2,1)S(1)}, bf16[128,128]{1,0:T(8,128)(2,1)}, u32[]{:S(2)}) copy-start(bf16[128,128]{1,0:T(8,128)(2,1)} %param.33) | copy-start | bytes 98308
  106.8 11.5 %all-to-all-start = ((bf16[6,4,24,128]{3,2,0,1:T(8,128)(2,1)}), bf16[6,4,24,128]{3,2,0,1:T(8,128)(2,1)S(1)}, u32[]{:S(2)}, u32[]{:S(2)}) async-start(bf16[6,4,24,128]{3,2,0,1:T(8,128)(2,1)} %copy.69), calls=%async_computation | async-start | bytes 294912 | tf_op jit(solution)/shard_map/all_to_all | solution.py:76
  112.3 0.8 copy-start.14
  119.0 13.3 %all-to-all-start.1 = ((bf16[6,1,96,128]{3,0,1,2:T(8,128)(2,1)}), bf16[6,1,96,128]{3,0,1,2:T(8,128)(2,1)S(1)}, u32[]{:S(2)}, u32[]{:S(2)}) async-start(bf16[6,1,96,128]{3,0,1,2:T(8,128)(2,1)} %copy.71), calls=%async_computation.1 | async-start | bytes 393216 | tf_op jit(solution)/shard_map/all_to_all | solution.py:75
  150.3 1.0 copy-start.2
  150.3 1.0 copy-start.5
  150.3 0.9 copy-start.6
  150.8 1.2 copy-start.7
  151.7 0.9 copy-start.8
  151.7 1.0 copy-start.9
Sparse Core Ops, SparseCore 0:
  10.8 90.4 all-reduce.1
where the time goes:
time: 161 us
  waiting for transfers between devices  94.6 us (59%)
  blocking collectives  26 us (16%)
  between operations  13.8 us (9%)
  starting transfers between devices  8.89 us (6%)
  matrix products  8.25 us (5%)
  other arithmetic  5.62 us (3%)
  local copies, waits for them, and re-layouts  3.72 us (2%)
    psum x1, waiting for transfers between devices, per_device(): total_sums = lax.psum(partial_sums, ('row', 'col'))  90.5 us
    all_gather x1, blocking collectives, per_device(): lax.all_gather(moved, 'col', axis=2, tiled=True)  16.7 us
    all_gather x1, blocking collectives, per_device(): lax.all_gather(right, 'row', axis=0, tiled=True)  9.33 us
    all_to_all x1, starting transfers between devices, per_device(): lax.all_to_all(shaped, 'col', split_axis=1, concat_axis=2, tiled=True)  5.49 us
    all_to_all x1, waiting for transfers between devices, per_device(): lax.all_to_all(shaped, 'col', split_axis=1, concat_axis=2, tiled=True)  4.11 us
    all_to_all x1, starting transfers between devices, per_device(): lax.all_to_all(lax.all_to_all(shaped, 'col', split_axis=1, concat_axis=2,...  3.36 us
  transfers between devices with their start and end apart: 3, of which 2 were waited for; matrix products, arithmetic and copies ran while one was open for 2% of the time, Pallas kernels for 0%

commit v1 on v0

v1 whole, which is shorter than its diff:
```python
import functools

import jax
import jax.numpy as jnp
from jax import lax
from jax.experimental import pallas as pl
from jax.experimental.pallas import tpu as pltpu
from jax.sharding import PartitionSpec as P

norm_epsilon = 1e-05
MESH = pl.DeviceIdType.MESH
SUM_TYPE = jnp.bfloat16


def layer_norm(values, gain_vec):
    centre = jnp.mean(values, axis=-1, keepdims=True)
    centered = values - centre
    variance = jnp.mean(centered * centered, axis=-1, keepdims=True)
    return centered * lax.rsqrt(variance + norm_epsilon) * gain_vec


def sigmoid(v):
    return 0.5 * jnp.tanh(0.5 * v) + 0.5


def mm(a, b):
    return jnp.dot(a, b, preferred_element_type=jnp.float32)


def mm_split(a, b):
    high = a.astype(jnp.bfloat16)
    low = (a - high.astype(jnp.float32)).astype(jnp.bfloat16)
    return mm(high, b) + mm(low, b)


def kernel(
    nrow, ncol, rb, cb, tokens,
    pair, feats, atom_token, atom_mask, token_mask,
    w_atom, gain_single, w_rows, w_cols, gain_pair,
    w_left, w_left_gate, w_right, w_right_gate, w_out_gate,
    gain_tri, w_out, gain_trans, w_up, w_upgate, w_down,
    out,
    feats_v, w_atom_v, w_rows_v, w_cols_v, w_l_v, w_r_v, w_og_v, w_out_v, w_up_v, w_ug_v, w_dn_v,
    left_pair, right_pair, part_sum, recv_row, col_sum, recv_col,
    row_term, col_term, left_blk, right_blk, tri, z_own, gate_own,
    load_sem, s1_send, s1_recv, s2_send, s2_recv, l_send, l_recv, r_send, r_recv,
):
    r = lax.axis_index("row")
    c = lax.axis_index("col")
    q = cb // rb
    ch = pair.shape[-1]

    barrier = pltpu.get_barrier_semaphore()
    for step in range(1, nrow * ncol):
        dr, dc = step // ncol, step % ncol
        pl.semaphore_signal(
            barrier,
            inc=1,
            device_id={"row": lax.rem(r + dr, nrow), "col": lax.rem(c + dc, ncol)},
            device_id_type=MESH,
        )

    moves = [
        (feats, feats_v),
        (w_atom, w_atom_v),
        (w_rows, w_rows_v),
        (w_cols, w_cols_v),
        (w_left, w_l_v.at[:, :ch]),
        (w_left_gate, w_l_v.at[:, ch:]),
        (w_right, w_r_v.at[:, :ch]),
        (w_right_gate, w_r_v.at[:, ch:]),
        (w_out_gate, w_og_v),
        (w_out, w_out_v),
        (w_up, w_up_v),
        (w_upgate, w_ug_v),
        (w_down, w_dn_v),
    ]
    loads = [pltpu.make_async_copy(a, b, load_sem.at[i]) for i, (a, b) in enumerate(moves)]
    for load in loads:
        load.start()

    loads[0].wait()
    atoms = feats_v.shape[0]
    ids = lax.broadcasted_iota(jnp.int32, (tokens, atoms), 0)
    member = (ids == atom_token[...].reshape(1, atoms)) & (atom_mask[...].reshape(1, atoms) > 0)
    member = jnp.where(member, 1.0, 0.0).astype(jnp.bfloat16)
    mine = mm(member, feats_v[...])
    part_sum[...] = mine.astype(SUM_TYPE)

    pl.semaphore_wait(barrier, nrow * ncol - 1)

    sum_copies = []
    for step in range(1, nrow):
        peer = lax.rem(r + step, nrow)
        cp = pltpu.make_async_remote_copy(
            src_ref=part_sum,
            dst_ref=recv_row.at[r],
            send_sem=s1_send.at[step],
            recv_sem=s1_recv.at[r],
            device_id={"row": peer},
            device_id_type=MESH,
        )
        cp.start()
        sum_copies.append(cp)

    own_rows = pl.ds(r * rb, rb)
    own_right = pltpu.make_async_copy(pair, right_pair.at[own_rows], r_recv.at[r])
    own_right.start()

    pair_copies = []
    local_copies = []
    for step in range(1, ncol + 1):
        target_col = lax.rem(c + step, ncol)
        for sub in range(q):
            target_row = c * q + sub
            src = pair if q == 1 else pair.at[:, pl.ds(sub * rb, rb), :]
            cp = pltpu.make_async_remote_copy(
                src_ref=src,
                dst_ref=left_pair.at[own_rows],
                send_sem=l_send.at[(step - 1) * q + sub],
                recv_sem=l_recv.at[r],
                device_id={"row": target_row, "col": target_col},
                device_id_type=MESH,
            )
            if step < ncol:
                cp.start()
                pair_copies.append(cp)
            else:
                local = pltpu.make_async_copy(src, left_pair.at[own_rows], l_recv.at[r])

                @pl.when(target_row == r)
                def _():
                    local.start()

                @pl.when(target_row != r)
                def _():
                    cp.start()

                local_copies.append((target_row, cp))
    for step in range(1, nrow):
        peer = lax.rem(r + step, nrow)
        cp = pltpu.make_async_remote_copy(
            src_ref=pair,
            dst_ref=right_pair.at[own_rows],
            send_sem=r_send.at[step],
            recv_sem=r_recv.at[r],
            device_id={"row": peer},
            device_id_type=MESH,
        )
        cp.start()
        pair_copies.append(cp)

    def wait_recv(buf, sem):
        pltpu.make_async_copy(buf, buf, sem).wait()

    total = mine
    for step in range(1, nrow):
        peer = lax.rem(r + nrow - step, nrow)
        wait_recv(recv_row.at[peer], s1_recv.at[peer])
        total = total + recv_row[peer].astype(jnp.float32)
    col_sum[...] = total.astype(SUM_TYPE)
    for step in range(1, ncol):
        peer = lax.rem(c + step, ncol)
        cp = pltpu.make_async_remote_copy(
            src_ref=col_sum,
            dst_ref=recv_col.at[c],
            send_sem=s2_send.at[step],
            recv_sem=s2_recv.at[c],
            device_id={"col": peer},
            device_id_type=MESH,
        )
        cp.start()
        sum_copies.append(cp)
    for load in loads[1:]:
        load.wait()
    for step in range(1, ncol):
        peer = lax.rem(c + ncol - step, ncol)
        wait_recv(recv_col.at[peer], s2_recv.at[peer])
        total = total + recv_col[peer].astype(jnp.float32)

    pooled = mm_split(total, w_atom_v[...])
    single = layer_norm(pooled, gain_single[...].reshape(1, -1))
    row_term[...] = mm_split(single, w_rows_v[...])
    col_term[...] = mm_split(single, w_cols_v[...])

    g_pair = gain_pair[...].reshape(1, ch)
    g_tri = gain_tri[...].reshape(1, ch)
    g_trans = gain_trans[...].reshape(1, ch)
    tri[...] = jnp.zeros_like(tri)

    def biased(src, base, cols, k, size):
        ct = col_term[cols, :]
        rows = [
            src[base + k + u].astype(jnp.float32) + (row_term[pl.ds(base + k + u, 1), :] + ct)
            for u in range(size)
        ]
        return jnp.concatenate(rows, axis=0)

    kc_left = max(1, min(rb, 192 // rb))
    kc_right = max(1, min(rb, 192 // cb))
    my_rows = pl.ds(pl.multiple_of(r * rb, 8), rb)
    my_cols = pl.ds(pl.multiple_of(c * cb, 8), cb)

    @pl.loop(0, nrow)
    def _(s):
        b = lax.rem(r + s, nrow)
        base = b * rb
        wait_recv(right_pair.at[pl.ds(base, rb)], r_recv.at[b])

        def right_chunk(n, _):
            k = n * kc_right
            z = biased(right_pair, base, my_cols, k, kc_right)
            normed = layer_norm(z, g_pair).astype(jnp.bfloat16)
            both = mm(normed, w_r_v[...])
            val = sigmoid(both[:, ch:]) * both[:, :ch]
            right_blk[pl.ds(k, kc_right)] = val.reshape(kc_right, cb, ch)

            @pl.when(s == 0)
            def _():
                z_own[pl.ds(k, kc_right)] = z.reshape(kc_right, cb, ch)
                gate = sigmoid(mm(normed, w_og_v[...]))
                gate_own[pl.ds(k, kc_right)] = gate.reshape(kc_right, cb, ch)

            return 0

        lax.fori_loop(0, rb // kc_right, right_chunk, 0)
        wait_recv(left_pair.at[pl.ds(base, rb)], l_recv.at[b])

        def left_chunk(n, _):
            k = n * kc_left
            z = biased(left_pair, base, my_rows, k, kc_left)
            normed = layer_norm(z, g_pair).astype(jnp.bfloat16)
            both = mm(normed, w_l_v[...])
            val = (sigmoid(both[:, ch:]) * both[:, :ch]).reshape(kc_left, rb, ch)
            for u in range(kc_left):
                left_blk[k + u] = val[u] * token_mask[base + k + u].astype(jnp.float32)
            return 0

        lax.fori_loop(0, rb // kc_left, left_chunk, 0)

        jb = 24 if cb % 24 == 0 else 8

        @pl.loop(0, rb // 8)
        def _(ig):
            @pl.loop(0, cb // jb)
            def _(jg):
                i0 = pl.multiple_of(ig * 8, 8)
                j0 = pl.multiple_of(jg * jb, 8)

                def step_k(k, acc):
                    rv = right_blk[k, pl.ds(j0, jb), :]
                    return tuple(
                        acc[u] + left_blk[k, pl.ds(i0 + u, 1), :] * rv for u in range(8)
                    )

                acc = tuple(tri[i0 + u, pl.ds(j0, jb), :] for u in range(8))
                acc = lax.fori_loop(0, rb, step_k, acc, unroll=4)
                for u in range(8):
                    tri[i0 + u, pl.ds(j0, jb), :] = acc[u]

    lane = lax.broadcasted_iota(jnp.int32, (cb, ch), 0)
    mask_cols = jnp.zeros((cb, ch), jnp.float32)
    for j in range(cb):
        mask_cols = jnp.where(lane == j, token_mask[c * cb + j].astype(jnp.float32), mask_cols)

    ic = max(1, min(rb, 192 // cb))
    hid = w_up_v.shape[1]

    @pl.loop(0, rb // ic)
    def _(n):
        i0 = n * ic
        weighed = jnp.concatenate(
            [
                tri[i0 + u] * (mask_cols * token_mask[r * rb + i0 + u].astype(jnp.float32))
                for u in range(ic)
            ],
            axis=0,
        )
        tri_normed = layer_norm(weighed, g_tri).astype(jnp.bfloat16)
        flat = (ic * cb, ch)
        z_second = z_own[pl.ds(i0, ic)].reshape(flat) + mm(tri_normed, w_out_v[...]) * gate_own[
            pl.ds(i0, ic)
        ].reshape(flat)
        trans_in = layer_norm(z_second, g_trans).astype(jnp.bfloat16)
        result = z_second
        half = hid // 2
        for h in range(2):
            cols = slice(h * half, (h + 1) * half)
            gate = mm(trans_in, w_ug_v[:, cols])
            up = mm(trans_in, w_up_v[:, cols])
            hidden = (gate * sigmoid(gate) * up).astype(jnp.bfloat16)
            result = result + mm(hidden, w_dn_v[cols, :])
        out[pl.ds(i0, ic)] = result.reshape(ic, cb, ch).astype(out.dtype)

    for cp in sum_copies + pair_copies:
        cp.wait_send()
    for target_row, cp in local_copies:

        @pl.when(target_row != r)
        def _():
            cp.wait_send()


def per_device(nrow, ncol, *args):
    pair, feats, token_mask = args[0], args[1], args[4]
    w_atom, w_rows, w_up = args[5], args[7], args[18]
    rb, cb, ch = pair.shape
    tokens = token_mask.shape[0]
    wide = w_atom.shape[1]
    hid = w_up.shape[1]
    bf, f32 = jnp.bfloat16, jnp.float32
    q = cb // rb
    anywhere = pl.BlockSpec(memory_space=pl.ANY)
    vmem = pl.BlockSpec(memory_space=pltpu.VMEM)
    smem = pl.BlockSpec(memory_space=pltpu.SMEM)
    specs = [anywhere] * 21
    for i in (2, 3, 6, 9, 15, 17):
        specs[i] = vmem
    specs[4] = smem
    dma = pltpu.SemaphoreType.DMA
    return pl.pallas_call(
        functools.partial(kernel, nrow, ncol, rb, cb, tokens),
        out_shape=jax.ShapeDtypeStruct(pair.shape, pair.dtype),
        in_specs=specs,
        out_specs=vmem,
        scratch_shapes=[
            pltpu.VMEM(feats.shape, bf),
            pltpu.VMEM(w_atom.shape, bf),
            pltpu.VMEM((wide, ch), bf),
            pltpu.VMEM((wide, ch), bf),
            pltpu.VMEM((ch, 2 * ch), bf),
            pltpu.VMEM((ch, 2 * ch), bf),
            pltpu.VMEM((ch, ch), bf),
            pltpu.VMEM((ch, ch), bf),
            pltpu.VMEM((ch, hid), bf),
            pltpu.VMEM((ch, hid), bf),
            pltpu.VMEM((hid, ch), bf),
            pltpu.VMEM((tokens, rb, ch), bf),
            pltpu.VMEM((tokens, cb, ch), bf),
            pltpu.VMEM((tokens, ch), SUM_TYPE),
            pltpu.VMEM((nrow, tokens, ch), SUM_TYPE),
            pltpu.VMEM((tokens, ch), SUM_TYPE),
            pltpu.VMEM((ncol, tokens, ch), SUM_TYPE),
            pltpu.VMEM((tokens, ch), f32),
            pltpu.VMEM((tokens, ch), f32),
            pltpu.VMEM((rb, rb, ch), f32),
            pltpu.VMEM((rb, cb, ch), f32),
            pltpu.VMEM((rb, cb, ch), f32),
            pltpu.VMEM((rb, cb, ch), f32),
            pltpu.VMEM((rb, cb, ch), f32),
            dma((13,)),
            dma((nrow,)),
            dma((nrow,)),
            dma((ncol,)),
            dma((ncol,)),
            dma((ncol * q,)),
            dma((nrow,)),
            dma((nrow,)),
            dma((nrow,)),
        ],
        compiler_params=pltpu.CompilerParams(
            collective_id=0, has_side_effects=True, vmem_limit_bytes=60 * 1024 * 1024
        ),
    )(*args)


def solution(mesh):
    nrow, ncol = mesh.shape["row"], mesh.shape["col"]
    placed = (
        P(("parts", "row"), "col", None),
        P(("parts", "row", "col"), None),
        P(("parts", "row", "col")),
        P(("parts", "row", "col")),
        P("parts"),
    ) + (P(),) * 16
    return jax.shard_map(
        functools.partial(per_device, nrow, ncol),
        mesh=mesh,
        in_specs=placed,
        out_specs=P(("parts", "row"), "col", None),
        check_vma=False,
    )
```

time: 161 us -> 40.3 us (0.25)
  waiting for transfers between devices: 94.6 us -> 0 us
  Pallas kernels: 0 us -> 38.5 us
  blocking collectives: 26 us -> 0 us
  between operations: 13.8 us -> 0.01 us
  starting transfers between devices: 8.89 us -> 0 us
  matrix products: 8.25 us -> 0 us
  other arithmetic: 5.62 us -> 0 us
  local copies, waits for them, and re-layouts: 3.72 us -> 1.59 us
    psum x1 -> x0, waiting for transfers between devices: 90.5 us -> none  [per_device(): total_sums = lax.psum(partial_sums, ('row', 'col'))]
    pallas_call x0 -> x1, Pallas kernels: none -> 38.5 us  [per_device(): pl.pallas_call(functools.partial(kernel, nrow, ncol, rb, cb, tokens), out...]
    all_gather x2 -> x0, blocking collectives: 26 us -> none  [the longest x1 16.7 us: per_device(): lax.all_gather(moved, 'col', axis=2, tiled=True)]
    all_to_all x2 -> x0, starting transfers between devices: 8.86 us -> none  [the longest x1 5.49 us: per_device(): lax.all_to_all(shaped, 'col', split_axis=1, concat_axis=2, tiled=True)]
    dot_general x13 -> x0, matrix products: 8.25 us -> none  [the longest x1 1.59 us: per_device(): partial_sums = jnp.dot(member, projected, precision=highest)]
    all_to_all x2 -> x0, waiting for transfers between devices: 4.11 us -> none  [the longest x1 4.11 us: per_device(): lax.all_to_all(shaped, 'col', split_axis=1, concat_axis=2, tiled=True)]
    reduce_sum x6 -> x0, other arithmetic: 3.07 us -> none  [the longest x4 1.9 us: layer_norm(): variance = jnp.mean(centered * centered, axis=-1, keepdims=True)]
  transfers between devices with their start and end apart: 3 -> 0, of which waited for: 2 -> 0; matrix products, arithmetic and copies ran while one was open for 2% -> 0% of each run, Pallas kernels for 0% -> 0%
where the time goes in v1:
time: 40.3 us; the launch traced here: 40.1 us
  Pallas kernels  38.5 us (96%)
  local copies, waits for them, and re-layouts  1.59 us (4%)
    pallas_call x1, Pallas kernels, per_device(): pl.pallas_call(functools.partial(kernel, nrow, ncol, rb, cb, tokens), out...  38.5 us
    unnamed x1, local copies, waits for them, and re-layouts  1.59 us

profile of v1, /device:TPU:0, one launch (start us, length us, event | category | flops | bytes accessed | tf_op | source)
XLA Modules:
  0.0 40.1 jit_solution(10322748270046352388)
XLA Ops:
  0.0 38.5 %shard_map.199 = bf16[24,24,128]{2,1,0:T(8,128)(2,1)} custom-call(bf16[24,24,128]{2,1,0:T(8,128)(2,1)} %pair.1, bf16[96,128]{1,0:T(8,128)(2,1)} %feats.1, s32[96]{0:T(128)} %atom_token.1, s32[96]{0:T(128)} %atom_mask.1, s32[96]{0:T(128)} %token_mask.1, bf16[128,384]{1,0:T(8,128)(2,1)} %w_atom.1, f32[384]{0:T(512)} %gain_single.1, bf16[384,128]{1,0:T(8,128)(2,1)} %w_rows.1, ...), custom_call_target="tpu_custom_call" | custom-call | tf_op jit(solution)/shard_map/pallas_call | solution.py:321
  38.5 1.6 %copy.23 = bf16[24,24,128]{2,1,0:T(8,128)(2,1)} copy(bf16[24,24,128]{2,1,0:T(8,128)(2,1)} %shard_map.199) | data formatting | bytes 294912

commit v2 on v1

v2 whole, which is shorter than its diff:
```python
import functools

import jax
import jax.numpy as jnp
from jax import lax
from jax.experimental import pallas as pl
from jax.experimental.pallas import tpu as pltpu
from jax.sharding import PartitionSpec as P

norm_epsilon = 1e-05
MESH = pl.DeviceIdType.MESH
SUM_TYPE = jnp.bfloat16


def layer_norm(values, gain_vec):
    centre = jnp.mean(values, axis=-1, keepdims=True)
    centered = values - centre
    variance = jnp.mean(centered * centered, axis=-1, keepdims=True)
    return centered * lax.rsqrt(variance + norm_epsilon) * gain_vec


def sigmoid(v):
    return 0.5 * jnp.tanh(0.5 * v) + 0.5


def mm(a, b):
    return jnp.dot(a, b, preferred_element_type=jnp.float32)


def mm_split(a, b):
    high = a.astype(jnp.bfloat16)
    low = (a - high.astype(jnp.float32)).astype(jnp.bfloat16)
    return mm(high, b) + mm(low, b)


def kernel(
    nrow, ncol, rb, cb, tokens, roomy,
    pair, feats, atom_token, atom_mask, token_mask,
    w_atom, gain_single, w_rows, w_cols, gain_pair,
    w_left, w_left_gate, w_right, w_right_gate, w_out_gate,
    gain_tri, w_out, gain_trans, w_up, w_upgate, w_down,
    out,
    feats_v, w_atom_v, w_rows_v, w_cols_v, w_l_v, w_r_v, w_og_v, w_out_v, w_up_v, w_ug_v, w_dn_v,
    blocks, part_sum, recv_col, col_sum, recv_row,
    row_term, col_term, left_blk, right_blk, z_own, gate_own, part_out, part_in,
    load_sem, s1_send, s1_recv, s2_send, s2_recv, up_send, down_send, z_recv, p_send, p_recv,
):
    r = lax.axis_index("row")
    c = lax.axis_index("col")
    q = cb // rb
    ch = pair.shape[-1]

    barrier = pltpu.get_barrier_semaphore()
    peers = [{"row": lax.rem(r + step, nrow)} for step in range(1, nrow)]
    peers += [{"col": lax.rem(c + step, ncol)} for step in range(1, ncol)]
    for peer in peers:
        pl.semaphore_signal(barrier, inc=1, device_id=peer, device_id_type=MESH)

    moves = [
        (feats, feats_v),
        (pair, blocks.at[c]),
        (w_atom, w_atom_v),
        (w_rows, w_rows_v),
        (w_cols, w_cols_v),
        (w_left, w_l_v.at[:, :ch]),
        (w_left_gate, w_l_v.at[:, ch:]),
        (w_right, w_r_v.at[:, :ch]),
        (w_right_gate, w_r_v.at[:, ch:]),
        (w_out_gate, w_og_v),
        (w_out, w_out_v),
        (w_up, w_up_v),
        (w_upgate, w_ug_v),
        (w_down, w_dn_v),
    ]
    loads = [pltpu.make_async_copy(a, b, load_sem.at[i]) for i, (a, b) in enumerate(moves)]
    for load in loads:
        load.start()

    loads[0].wait()
    atoms = feats_v.shape[0]
    ids = lax.broadcasted_iota(jnp.int32, (tokens, atoms), 0)
    member = (ids == atom_token[...].reshape(1, atoms)) & (atom_mask[...].reshape(1, atoms) > 0)
    member = jnp.where(member, 1.0, 0.0).astype(jnp.bfloat16)
    mine = mm(member, feats_v[...])
    part_sum[...] = mine.astype(SUM_TYPE)

    pl.semaphore_wait(barrier, nrow + ncol - 2)

    def wait_recv(buf, sem):
        pltpu.make_async_copy(buf, buf, sem).wait()

    copies = []
    for step in range(1, ncol):
        cp = pltpu.make_async_remote_copy(
            src_ref=part_sum,
            dst_ref=recv_col.at[c],
            send_sem=s1_send.at[step],
            recv_sem=s1_recv.at[c],
            device_id={"col": lax.rem(c + step, ncol)},
            device_id_type=MESH,
        )
        cp.start()
        copies.append(cp)

    def relay(b, way, src=None):
        return pltpu.make_async_remote_copy(
            src_ref=blocks.at[b] if src is None else src,
            dst_ref=blocks.at[b],
            send_sem=(up_send if way > 0 else down_send).at[b],
            recv_sem=z_recv.at[b],
            device_id={"col": lax.rem(c + way + ncol, ncol)},
            device_id_type=MESH,
        )

    @pl.when(c < ncol - 1)
    def _():
        relay(c, 1, pair).start()

    @pl.when(c > 0)
    def _():
        relay(c, -1, pair).start()

    def forward(s):
        @pl.when((c >= s) & (c < ncol - 1))
        def _():
            b = lax.rem(c - s + ncol, ncol)
            wait_recv(blocks.at[b], z_recv.at[b])
            relay(b, 1).start()

        @pl.when((c + s < ncol) & (c > 0))
        def _():
            b = lax.rem(c + s, ncol)
            wait_recv(blocks.at[b], z_recv.at[b])
            relay(b, -1).start()

    total = mine
    for step in range(1, ncol):
        peer = lax.rem(c + ncol - step, ncol)
        wait_recv(recv_col.at[peer], s1_recv.at[peer])
        total = total + recv_col[peer].astype(jnp.float32)
    col_sum[...] = total.astype(SUM_TYPE)
    for step in range(1, nrow):
        cp = pltpu.make_async_remote_copy(
            src_ref=col_sum,
            dst_ref=recv_row.at[r],
            send_sem=s2_send.at[step],
            recv_sem=s2_recv.at[r],
            device_id={"row": lax.rem(r + step, nrow)},
            device_id_type=MESH,
        )
        cp.start()
        copies.append(cp)
    for load in loads[1:]:
        load.wait()
    for step in range(1, nrow):
        peer = lax.rem(r + nrow - step, nrow)
        wait_recv(recv_row.at[peer], s2_recv.at[peer])
        total = total + recv_row[peer].astype(jnp.float32)
    forward(1)

    pooled = mm_split(total, w_atom_v[...])
    single = layer_norm(pooled, gain_single[...].reshape(1, -1))
    row_term[...] = mm_split(single, w_rows_v[...])
    col_term[...] = mm_split(single, w_cols_v[...])

    g_pair = gain_pair[...].reshape(1, ch)
    g_tri = gain_tri[...].reshape(1, ch)
    g_trans = gain_trans[...].reshape(1, ch)
    kc = max(1, min(rb, 192 // cb))
    jb = cb if cb <= 32 else 32

    def biased(b, k):
        ct = col_term[pl.ds(pl.multiple_of(b * cb, 8), cb), :]
        rows = [
            blocks[b, k + u].astype(jnp.float32) + (row_term[pl.ds(r * rb + k + u, 1), :] + ct)
            for u in range(kc)
        ]
        return jnp.concatenate(rows, axis=0)

    def gated(normed, weights):
        both = mm(normed, weights)
        return (sigmoid(both[:, ch:]) * both[:, :ch]).reshape(kc, cb, ch)

    def piece(target, slot):
        return pltpu.make_async_remote_copy(
            src_ref=part_out.at[slot],
            dst_ref=part_in.at[r],
            send_sem=p_send.at[target],
            recv_sem=p_recv.at[r],
            device_id={"row": target},
            device_id_type=MESH,
        )

    def partial(b):
        for sub in range(q):
            target = b * q + sub
            slot = target if roomy else sub

            @pl.loop(0, rb // 8)
            def _(ig):
                i0 = pl.multiple_of(ig * 8, 8)
                for j0 in range(0, cb, jb):

                    def step_k(k, acc):
                        rv = right_blk[k, j0 : j0 + jb, :]
                        return tuple(
                            acc[u] + left_blk[k, pl.ds(sub * rb + i0 + u, 1), :] * rv
                            for u in range(8)
                        )

                    zero = jnp.zeros((jb, ch), jnp.float32)
                    acc = lax.fori_loop(0, rb, step_k, (zero,) * 8, unroll=4)
                    for u in range(8):
                        part_out[slot, i0 + u, j0 : j0 + jb, :] = acc[u].astype(part_out.dtype)

            @pl.when(target == r)
            def _():
                part_in[r] = part_out[slot]

            @pl.when(target != r)
            def _():
                cp = piece(target, slot)
                cp.start()
                if not roomy:
                    cp.wait_send()

    @pl.loop(0, rb // kc)
    def _(n):
        k = n * kc
        z = biased(c, k)
        normed = layer_norm(z, g_pair).astype(jnp.bfloat16)
        z_own[pl.ds(k, kc)] = z.reshape(kc, cb, ch)
        left_blk[pl.ds(k, kc)] = gated(normed, w_l_v[...])
        right = gated(normed, w_r_v[...])
        for u in range(kc):
            right_blk[k + u] = right[u] * token_mask[r * rb + k + u].astype(jnp.float32)
        gate_own[pl.ds(k, kc)] = sigmoid(mm(normed, w_og_v[...])).reshape(kc, cb, ch)

    partial(c)

    @pl.loop(1, ncol)
    def _(s):
        forward(s + 1)

        @pl.loop(0, 2)
        def _(side):
            b = c + (2 * side - 1) * s

            @pl.when((b >= 0) & (b < ncol))
            def _():
                inside = lax.rem(b + ncol, ncol)

                @pl.when(((side == 0) & (c == ncol - 1)) | ((side == 1) & (c == 0)))
                def _():
                    wait_recv(blocks.at[inside], z_recv.at[inside])

                @pl.loop(0, rb // kc)
                def _(n):
                    k = n * kc
                    normed = layer_norm(biased(inside, k), g_pair).astype(jnp.bfloat16)
                    left_blk[pl.ds(k, kc)] = gated(normed, w_l_v[...])

                partial(inside)

    lane = lax.broadcasted_iota(jnp.int32, (cb, ch), 0)
    mask_cols = jnp.zeros((cb, ch), jnp.float32)
    for j in range(cb):
        mask_cols = jnp.where(lane == j, token_mask[c * cb + j].astype(jnp.float32), mask_cols)

    for step in range(1, nrow):
        peer = lax.rem(r + step, nrow)
        wait_recv(part_in.at[peer], p_recv.at[peer])

    hid = w_up_v.shape[1]

    @pl.loop(0, rb // kc)
    def _(n):
        i0 = n * kc
        rows = []
        for u in range(kc):
            row = part_in[0, i0 + u].astype(jnp.float32)
            for peer in range(1, nrow):
                row = row + part_in[peer, i0 + u].astype(jnp.float32)
            rows.append(row * (mask_cols * token_mask[r * rb + i0 + u].astype(jnp.float32)))
        tri_normed = layer_norm(jnp.concatenate(rows, axis=0), g_tri).astype(jnp.bfloat16)
        flat = (kc * cb, ch)
        z_second = z_own[pl.ds(i0, kc)].reshape(flat) + mm(tri_normed, w_out_v[...]) * gate_own[
            pl.ds(i0, kc)
        ].reshape(flat)
        trans_in = layer_norm(z_second, g_trans).astype(jnp.bfloat16)
        result = z_second
        half = hid // 2
        for h in range(2):
            cols = slice(h * half, (h + 1) * half)
            gate = mm(trans_in, w_ug_v[:, cols])
            up = mm(trans_in, w_up_v[:, cols])
            hidden = (gate * sigmoid(gate) * up).astype(jnp.bfloat16)
            result = result + mm(hidden, w_dn_v[cols, :])
        out[pl.ds(i0, kc)] = result.reshape(kc, cb, ch).astype(out.dtype)

    for cp in copies:
        cp.wait_send()
    for b in range(ncol):

        @pl.when((c >= b) & (c < ncol - 1))
        def _():
            relay(b, 1).wait_send()

        @pl.when((c <= b) & (c > 0))
        def _():
            relay(b, -1).wait_send()

    if roomy:
        for step in range(1, nrow):
            target = lax.rem(r + step, nrow)
            piece(target, target).wait_send()


def per_device(nrow, ncol, *args):
    pair, feats, token_mask = args[0], args[1], args[4]
    w_atom, w_rows, w_up = args[5], args[7], args[18]
    rb, cb, ch = pair.shape
    tokens = token_mask.shape[0]
    wide = w_atom.shape[1]
    hid = w_up.shape[1]
    bf, f32 = jnp.bfloat16, jnp.float32
    q = cb // rb
    roomy = nrow * rb * cb * ch <= 1 << 22
    anywhere = pl.BlockSpec(memory_space=pl.ANY)
    vmem = pl.BlockSpec(memory_space=pltpu.VMEM)
    smem = pl.BlockSpec(memory_space=pltpu.SMEM)
    specs = [anywhere] * 21
    for i in (2, 3, 6, 9, 15, 17):
        specs[i] = vmem
    specs[4] = smem
    dma = pltpu.SemaphoreType.DMA
    return pl.pallas_call(
        functools.partial(kernel, nrow, ncol, rb, cb, tokens, roomy),
        out_shape=jax.ShapeDtypeStruct(pair.shape, pair.dtype),
        in_specs=specs,
        out_specs=vmem,
        scratch_shapes=[
            pltpu.VMEM(feats.shape, bf),
            pltpu.VMEM(w_atom.shape, bf),
            pltpu.VMEM((wide, ch), bf),
            pltpu.VMEM((wide, ch), bf),
            pltpu.VMEM((ch, 2 * ch), bf),
            pltpu.VMEM((ch, 2 * ch), bf),
            pltpu.VMEM((ch, ch), bf),
            pltpu.VMEM((ch, ch), bf),
            pltpu.VMEM((ch, hid), bf),
            pltpu.VMEM((ch, hid), bf),
            pltpu.VMEM((hid, ch), bf),
            pltpu.VMEM((ncol, rb, cb, ch), bf),
            pltpu.VMEM((tokens, ch), SUM_TYPE),
            pltpu.VMEM((ncol, tokens, ch), SUM_TYPE),
            pltpu.VMEM((tokens, ch), SUM_TYPE),
            pltpu.VMEM((nrow, tokens, ch), SUM_TYPE),
            pltpu.VMEM((tokens, ch), f32),
            pltpu.VMEM((tokens, ch), f32),
            pltpu.VMEM((rb, cb, ch), f32),
            pltpu.VMEM((rb, cb, ch), f32),
            pltpu.VMEM((rb, cb, ch), f32),
            pltpu.VMEM((rb, cb, ch), f32),
            pltpu.VMEM((nrow if roomy else q, rb, cb, ch), bf),
            pltpu.VMEM((nrow, rb, cb, ch), bf),
            dma((14,)),
            dma((ncol,)),
            dma((ncol,)),
            dma((nrow,)),
            dma((nrow,)),
            dma((ncol,)),
            dma((ncol,)),
            dma((ncol,)),
            dma((nrow,)),
            dma((nrow,)),
        ],
        compiler_params=pltpu.CompilerParams(
            collective_id=0, has_side_effects=True, vmem_limit_bytes=60 * 1024 * 1024
        ),
    )(*args)


def solution(mesh):
    nrow, ncol = mesh.shape["row"], mesh.shape["col"]
    placed = (
        P(("parts", "row"), "col", None),
        P(("parts", "row", "col"), None),
        P(("parts", "row", "col")),
        P(("parts", "row", "col")),
        P("parts"),
    ) + (P(),) * 16
    return jax.shard_map(
        functools.partial(per_device, nrow, ncol),
        mesh=mesh,
        in_specs=placed,
        out_specs=P(("parts", "row"), "col", None),
        check_vma=False,
    )
```

time: 40.3 us -> 32.8 us (0.81)
  the two profiles are of different devices: /device:TPU:0 before, /device:TPU:5 now
where the time goes in v2:
time: 32.8 us; the launch traced here: 32.5 us
  Pallas kernels  30.9 us (94%)
  local copies, waits for them, and re-layouts  1.59 us (5%)
    pallas_call x1, Pallas kernels, per_device(): pl.pallas_call(functools.partial(kernel, nrow, ncol, rb, cb, tokens, room...  30.9 us
    unnamed x1, local copies, waits for them, and re-layouts  1.59 us

profile of v2, /device:TPU:5, one launch (start us, length us, event | category | flops | bytes accessed | tf_op | source)
XLA Modules:
  0.0 32.5 jit_solution(13384348120809771844)
XLA Ops:
  0.0 30.9 %shard_map.199 = bf16[24,24,128]{2,1,0:T(8,128)(2,1)} custom-call(bf16[24,24,128]{2,1,0:T(8,128)(2,1)} %pair.1, bf16[96,128]{1,0:T(8,128)(2,1)} %feats.1, s32[96]{0:T(128)} %atom_token.1, s32[96]{0:T(128)} %atom_mask.1, s32[96]{0:T(128)} %token_mask.1, bf16[128,384]{1,0:T(8,128)(2,1)} %w_atom.1, f32[384]{0:T(512)} %gain_single.1, bf16[384,128]{1,0:T(8,128)(2,1)} %w_rows.1, ...), custom_call_target="tpu_custom_call" | custom-call | tf_op jit(solution)/shard_map/pallas_call | solution.py:337
  30.9 1.6 %copy.23 = bf16[24,24,128]{2,1,0:T(8,128)(2,1)} copy(bf16[24,24,128]{2,1,0:T(8,128)(2,1)} %shard_map.199) | data formatting | bytes 294912

commit v3 on v2

--- a/solution.py
+++ b/solution.py
@@ -90,13 +90,13 @@
         pltpu.make_async_copy(buf, buf, sem).wait()
 
     copies = []
-    for step in range(1, ncol):
+    for step in range(1, nrow):
         cp = pltpu.make_async_remote_copy(
             src_ref=part_sum,
-            dst_ref=recv_col.at[c],
+            dst_ref=recv_row.at[r],
             send_sem=s1_send.at[step],
-            recv_sem=s1_recv.at[c],
-            device_id={"col": lax.rem(c + step, ncol)},
+            recv_sem=s1_recv.at[r],
+            device_id={"row": lax.rem(r + step, nrow)},
             device_id_type=MESH,
         )
         cp.start()
@@ -134,29 +134,29 @@
             relay(b, -1).start()
 
     total = mine
+    for step in range(1, nrow):
+        peer = lax.rem(r + nrow - step, nrow)
+        wait_recv(recv_row.at[peer], s1_recv.at[peer])
+        total = total + recv_row[peer].astype(jnp.float32)
+    col_sum[...] = total.astype(SUM_TYPE)
     for step in range(1, ncol):
-        peer = lax.rem(c + ncol - step, ncol)
-        wait_recv(recv_col.at[peer], s1_recv.at[peer])
-        total = total + recv_col[peer].astype(jnp.float32)
-    col_sum[...] = total.astype(SUM_TYPE)
-    for step in range(1, nrow):
         cp = pltpu.make_async_remote_copy(
             src_ref=col_sum,
-            dst_ref=recv_row.at[r],
+            dst_ref=recv_col.at[c],
             send_sem=s2_send.at[step],
-            recv_sem=s2_recv.at[r],
-            device_id={"row": lax.rem(r + step, nrow)},
+            recv_sem=s2_recv.at[c],
+            device_id={"col": lax.rem(c + step, ncol)},
             device_id_type=MESH,
         )
         cp.start()
         copies.append(cp)
+    forward(1)
     for load in loads[1:]:
         load.wait()
-    for step in range(1, nrow):
-        peer = lax.rem(r + nrow - step, nrow)
-        wait_recv(recv_row.at[peer], s2_recv.at[peer])
-        total = total + recv_row[peer].astype(jnp.float32)
-    forward(1)
+    for step in range(1, ncol):
+        peer = lax.rem(c + ncol - step, ncol)
+        wait_recv(recv_col.at[peer], s2_recv.at[peer])
+        total = total + recv_col[peer].astype(jnp.float32)
 
     pooled = mm_split(total, w_atom_v[...])
     single = layer_norm(pooled, gain_single[...].reshape(1, -1))
@@ -365,10 +365,10 @@
             pltpu.VMEM((nrow if roomy else q, rb, cb, ch), bf),
             pltpu.VMEM((nrow, rb, cb, ch), bf),
             dma((14,)),
-            dma((ncol,)),
-            dma((ncol,)),
             dma((nrow,)),
             dma((nrow,)),
+            dma((ncol,)),
+            dma((ncol,)),
             dma((ncol,)),
             dma((ncol,)),
             dma((ncol,)),

time: 32.8 us -> 30.3 us (0.924)
  Pallas kernels: 30.9 us -> 28.4 us
    pallas_call x1, Pallas kernels: 30.9 us -> 28.4 us  [per_device(): pl.pallas_call(functools.partial(kernel, nrow, ncol, rb, cb, tokens, room...]
where the time goes in v3:
time: 30.3 us; the launch traced here: 30 us
  Pallas kernels  28.4 us (94%)
  local copies, waits for them, and re-layouts  1.59 us (5%)
    pallas_call x1, Pallas kernels, per_device(): pl.pallas_call(functools.partial(kernel, nrow, ncol, rb, cb, tokens, room...  28.4 us
    unnamed x1, local copies, waits for them, and re-layouts  1.59 us

profile of v3, /device:TPU:5, one launch (start us, length us, event | category | flops | bytes accessed | tf_op | source)
XLA Modules:
  0.0 30.0 jit_solution(13076636789711196628)
XLA Ops:
  0.0 28.4 %shard_map.199 = bf16[24,24,128]{2,1,0:T(8,128)(2,1)} custom-call(bf16[24,24,128]{2,1,0:T(8,128)(2,1)} %pair.1, bf16[96,128]{1,0:T(8,128)(2,1)} %feats.1, s32[96]{0:T(128)} %atom_token.1, s32[96]{0:T(128)} %atom_mask.1, s32[96]{0:T(128)} %token_mask.1, bf16[128,384]{1,0:T(8,128)(2,1)} %w_atom.1, f32[384]{0:T(512)} %gain_single.1, bf16[384,128]{1,0:T(8,128)(2,1)} %w_rows.1, ...), custom_call_target="tpu_custom_call" | custom-call | tf_op jit(solution)/shard_map/pallas_call | solution.py:337
  28.4 1.6 %copy.23 = bf16[24,24,128]{2,1,0:T(8,128)(2,1)} copy(bf16[24,24,128]{2,1,0:T(8,128)(2,1)} %shard_map.199) | data formatting | bytes 294912

commit v4 on v3

--- a/solution.py
+++ b/solution.py
@@ -181,12 +181,13 @@
         both = mm(normed, weights)
         return (sigmoid(both[:, ch:]) * both[:, :ch]).reshape(kc, cb, ch)
 
-    def piece(target, slot):
+    def piece(target, slot, g):
+        group = pl.ds(g * 8, 8)
         return pltpu.make_async_remote_copy(
-            src_ref=part_out.at[slot],
-            dst_ref=part_in.at[r],
-            send_sem=p_send.at[target],
-            recv_sem=p_recv.at[r],
+            src_ref=part_out.at[slot, group],
+            dst_ref=part_in.at[r, group],
+            send_sem=p_send.at[target, g],
+            recv_sem=p_recv.at[r, g],
             device_id={"row": target},
             device_id_type=MESH,
         )
@@ -213,16 +214,16 @@
                     for u in range(8):
                         part_out[slot, i0 + u, j0 : j0 + jb, :] = acc[u].astype(part_out.dtype)
 
-            @pl.when(target == r)
-            def _():
-                part_in[r] = part_out[slot]
-
-            @pl.when(target != r)
-            def _():
-                cp = piece(target, slot)
-                cp.start()
-                if not roomy:
-                    cp.wait_send()
+                @pl.when(target == r)
+                def _():
+                    part_in[r, pl.ds(i0, 8)] = part_out[slot, pl.ds(i0, 8)]
+
+                @pl.when(target != r)
+                def _():
+                    cp = piece(target, slot, ig)
+                    cp.start()
+                    if not roomy:
+                        cp.wait_send()
 
     @pl.loop(0, rb // kc)
     def _(n):
@@ -267,15 +268,22 @@
     for j in range(cb):
         mask_cols = jnp.where(lane == j, token_mask[c * cb + j].astype(jnp.float32), mask_cols)
 
-    for step in range(1, nrow):
-        peer = lax.rem(r + step, nrow)
-        wait_recv(part_in.at[peer], p_recv.at[peer])
+    def group_arrived(g):
+        for step in range(1, nrow):
+            peer = lax.rem(r + step, nrow)
+            wait_recv(part_in.at[peer, pl.ds(g * 8, 8)], p_recv.at[peer, g])
+
+    if kc != 8:
+        for g in range(rb // 8):
+            group_arrived(g)
 
     hid = w_up_v.shape[1]
 
     @pl.loop(0, rb // kc)
     def _(n):
         i0 = n * kc
+        if kc == 8:
+            group_arrived(n)
         rows = []
         for u in range(kc):
             row = part_in[0, i0 + u].astype(jnp.float32)
@@ -313,7 +321,8 @@
     if roomy:
         for step in range(1, nrow):
             target = lax.rem(r + step, nrow)
-            piece(target, target).wait_send()
+            for g in range(rb // 8):
+                piece(target, target, g).wait_send()
 
 
 def per_device(nrow, ncol, *args):
@@ -372,8 +381,8 @@
             dma((ncol,)),
             dma((ncol,)),
             dma((ncol,)),
-            dma((nrow,)),
-            dma((nrow,)),
+            dma((nrow, rb // 8)),
+            dma((nrow, rb // 8)),
         ],
         compiler_params=pltpu.CompilerParams(
             collective_id=0, has_side_effects=True, vmem_limit_bytes=60 * 1024 * 1024

time: 30.3 us -> 28.9 us (0.954)
  Pallas kernels: 28.4 us -> 27.2 us
    pallas_call x1, Pallas kernels: 28.4 us -> 27.2 us  [per_device(): pl.pallas_call(functools.partial(kernel, nrow, ncol, rb, cb, tokens, room...]
where the time goes in v4:
time: 28.9 us; the launch traced here: 28.7 us
  Pallas kernels  27.2 us (94%)
  local copies, waits for them, and re-layouts  1.59 us (6%)
    pallas_call x1, Pallas kernels, per_device(): pl.pallas_call(functools.partial(kernel, nrow, ncol, rb, cb, tokens, room...  27.2 us
    unnamed x1, local copies, waits for them, and re-layouts  1.59 us

profile of v4, /device:TPU:5, one launch (start us, length us, event | category | flops | bytes accessed | tf_op | source)
XLA Modules:
  0.0 28.7 jit_solution(14911466947235413109)
XLA Ops:
  0.0 27.2 %shard_map.199 = bf16[24,24,128]{2,1,0:T(8,128)(2,1)} custom-call(bf16[24,24,128]{2,1,0:T(8,128)(2,1)} %pair.1, bf16[96,128]{1,0:T(8,128)(2,1)} %feats.1, s32[96]{0:T(128)} %atom_token.1, s32[96]{0:T(128)} %atom_mask.1, s32[96]{0:T(128)} %token_mask.1, bf16[128,384]{1,0:T(8,128)(2,1)} %w_atom.1, f32[384]{0:T(512)} %gain_single.1, bf16[384,128]{1,0:T(8,128)(2,1)} %w_rows.1, ...), custom_call_target="tpu_custom_call" | custom-call | tf_op jit(solution)/shard_map/pallas_call | solution.py:346
  27.2 1.6 %copy.23 = bf16[24,24,128]{2,1,0:T(8,128)(2,1)} copy(bf16[24,24,128]{2,1,0:T(8,128)(2,1)} %shard_map.199) | data formatting | bytes 294912
